TPU v7x, 32 devices: a whole 2x2x4 slice. The times are simulated.
32 devices in a mesh: groups: 1, seq: 4 (over z), tensor: 4 (over y, x), section: 2 (over core).
Axes of the slice: x: 2, y: 2, z: 4, core: 2. Of those that a mesh axis runs over, the one named last changes fastest.
Arguments:
- prompts: bfloat16 [1024, 8192], P(('groups', 'seq', 'section')), may hold values from -6 to 6
- kv_weight: bfloat16 [8192, 2, 1024], P(('seq', 'section'), None, 'tensor'), may hold values from -0.0625 to 0.0625
- lengths: int32 [64], P('groups'), may hold values from 1 to 512, 1024 in all
- piece_owner: int32 [32], P('groups'), may hold values from 0 to 7, as said below
- piece_slot: int32 [32], P('groups'), may hold values from 0 to 7, as said below
- queries: bfloat16 [256, 8192], P('groups', 'tensor'), may hold values from -128 to 128
- decode_key_value: bfloat16 [256, 2, 1024], P('groups', None, 'tensor'), may hold values from -16 to 16
Outputs:
- cache: bfloat16 [2048, 2, 1024], P(('groups', 'seq', 'section'), None, 'tensor')
- attended: bfloat16 [256, 8192], P('groups', 'tensor')
Inputs may be any that keep to these rules, and one draw needn't show every extreme that they name: `piece_owner`: the pieces of one device (4 aligned pieces in a row) go to distinct owners; an owner receives at most 8 pieces, and some owner receives exactly 8. `piece_slot`: the pieces of one owner hold distinct slots; an owner with n pieces uses slots 0 to n - 1.
All inputs are finite; a program needn't handle non-finite values.
Results may differ from a plain program's by a relative error of at most 0.0015.
The roundings to bfloat16 on the way count: a program that leaves them out, or rounds other values in their place, can miss the bound.
Values may be sent and summed in bfloat16 or wider, within the bound.
A program may use at most 64 MiB of HBM per device.

v0:
```python
import jax
import jax.numpy as jnp
from jax import lax
from jax.sharding import PartitionSpec as P

HEAD_SIZE = 128
DECODE_STEPS = 4


masked_value = -1e30


def partial_softmax(scores, allowed):
    highest = jnp.max(jnp.where(allowed, scores, masked_value), axis=-1)
    weights = jnp.where(allowed, jnp.exp(scores - highest[..., None]), 0.0)
    return (highest, jnp.sum(weights, axis=-1), weights.astype(jnp.bfloat16))


def join_parts(first, second):
    top = jnp.maximum(first[0], second[0])
    left = jnp.exp(first[0] - top)
    right = jnp.exp(second[0] - top)
    return (
        top,
        first[1] * left + second[1] * right,
        first[2] * left[..., None] + second[2] * right[..., None],
    )


def per_device(prompts, kv_weight, lengths, piece_owner, piece_slot, queries, decode_key_value):
    shards = lax.axis_size(("seq", "section"))
    sender = lax.axis_index(("seq", "section"))
    tok_rows = prompts.shape[0]
    local_kv = kv_weight.shape[2]
    per_sender = shards // 2
    piece_len = tok_rows // per_sender
    cache_block = lax.all_gather(kv_weight, ("seq", "section"), axis=0, tiled=True)
    flat = cache_block.reshape(cache_block.shape[0], 2 * local_kv)
    summed = jnp.dot(prompts, flat, preferred_element_type=jnp.float32)
    fresh_entries = summed.astype(jnp.bfloat16).reshape(tok_rows, 2, local_kv)
    pieces = fresh_entries.reshape(per_sender, piece_len * 2 * local_kv)
    my_owners = lax.dynamic_slice_in_dim(piece_owner, sender * per_sender, per_sender)
    owner_range = jnp.arange(shards, dtype=jnp.int32)
    targets = (owner_range[:, None] == my_owners[None, :]).astype(jnp.bfloat16)
    outgoing = jnp.dot(targets, pieces, preferred_element_type=jnp.float32).astype(jnp.bfloat16)
    arrived = lax.all_to_all(outgoing, ("seq", "section"), split_axis=0, concat_axis=0, tiled=True)
    piece_ids = jnp.arange(piece_owner.shape[0], dtype=jnp.int32)
    matched = (
        (piece_owner == sender)[None, :] & (piece_slot[None, :] == owner_range[:, None])
    ).astype(jnp.int32)
    from_sender = jnp.sum(matched.reshape(shards, shards, per_sender), axis=2).astype(jnp.bfloat16)
    cache_local = jnp.dot(from_sender, arrived, preferred_element_type=jnp.float32).astype(
        jnp.bfloat16
    )
    cache_local = cache_local.reshape(shards * piece_len, 2, local_kv)
    has_piece = jnp.sum(matched, axis=1)
    first_token = jnp.sum(matched * piece_ids[None, :], axis=1) * piece_len
    slot_token = (first_token[:, None] + jnp.arange(piece_len, dtype=jnp.int32)[None, :]).reshape(
        -1
    )
    ends = jnp.cumsum(lengths)
    token_request = jnp.sum((slot_token[:, None] >= ends[None, :]).astype(jnp.int32), axis=1)
    filled = jnp.repeat(has_piece > 0, piece_len)
    slot_request = jnp.where(filled, token_request, -1)
    rows = queries.shape[0]
    kv_heads = local_kv // HEAD_SIZE
    query_group = queries.shape[1] // (kv_heads * HEAD_SIZE)
    scale = HEAD_SIZE ** (-0.5)
    asked_rows = queries.reshape(rows, kv_heads, query_group, HEAD_SIZE)
    cache_keys = cache_local[:, 0].reshape(-1, kv_heads, HEAD_SIZE)
    cache_values = cache_local[:, 1].reshape(-1, kv_heads, HEAD_SIZE)
    scores = (
        jnp.einsum("rgjd,cgd->rgjc", asked_rows, cache_keys, preferred_element_type=jnp.float32)
        * scale
    )
    row_request = jnp.arange(rows, dtype=jnp.int32) // DECODE_STEPS
    allowed = (slot_request[None, :] == row_request[:, None])[:, None, None, :]
    highest, total, weights = partial_softmax(scores, allowed)
    weighted = jnp.einsum(
        "rgjc,cgd->rgjd", weights, cache_values, preferred_element_type=jnp.float32
    )
    requests = rows // DECODE_STEPS
    asked_fresh_rows = queries.reshape(requests, DECODE_STEPS, kv_heads, query_group, HEAD_SIZE)
    fresh_key_rows = decode_key_value[:, 0].reshape(requests, DECODE_STEPS, kv_heads, HEAD_SIZE)
    fresh_value_rows = decode_key_value[:, 1].reshape(requests, DECODE_STEPS, kv_heads, HEAD_SIZE)
    new_scores = (
        jnp.einsum(
            "rtgjd,rsgd->rtgjs",
            asked_fresh_rows,
            fresh_key_rows,
            preferred_element_type=jnp.float32,
        )
        * scale
    )
    steps_range = jnp.arange(DECODE_STEPS, dtype=jnp.int32)
    causal = (steps_range[:, None] >= steps_range[None, :])[None, :, None, None, :]
    fresh_maximum, fresh_total_sum, new_weights = partial_softmax(new_scores, causal)
    fresh_weight_sum = jnp.einsum(
        "rtgjs,rsgd->rtgjd", new_weights, fresh_value_rows, preferred_element_type=jnp.float32
    )
    new_part = (
        fresh_maximum.reshape(rows, kv_heads, query_group),
        fresh_total_sum.reshape(rows, kv_heads, query_group),
        fresh_weight_sum.reshape(rows, kv_heads, query_group, HEAD_SIZE),
    )
    top = lax.pmax(highest, ("seq", "section"))
    group_factor = jnp.exp(highest - top)
    total_sum, weighted_sum = lax.psum(
        (total * group_factor, weighted * group_factor[..., None]), ("seq", "section")
    )
    owners_part = (top, total_sum, weighted_sum)
    final = join_parts(owners_part, new_part)
    attended = (
        (final[2] / final[1][..., None])
        .astype(jnp.bfloat16)
        .reshape(rows, kv_heads * query_group * HEAD_SIZE)
    )
    return (cache_local, attended)


def solution(mesh):
    placed = (
        P(("groups", "seq", "section"), None),
        P(("seq", "section"), None, "tensor"),
        P("groups"),
        P("groups"),
        P("groups"),
        P("groups", "tensor"),
        P("groups", None, "tensor"),
    )
    return jax.shard_map(
        per_device,
        mesh=mesh,
        in_specs=placed,
        out_specs=(P(("groups", "seq", "section"), None, "tensor"), P("groups", "tensor")),
        check_vma=False,
    )
```

profile of v0, /device:TPU:9, one launch (start us, length us, event | category | flops | bytes accessed | tf_op | source)
XLA Modules:
  0.0 238.8 jit_solution(14149758327833677125)
XLA Ops:
  7.2 0.0 copy-start
  7.2 0.0 all-gather.2.cloned.1.call-start
  7.2 0.7 all-gather.2.cloned.1.call-update
  7.9 0.7 eq.60
  8.7 0.1 copy.72
  8.7 0.7 dynamic_slice.3
  9.5 0.7 broadcast_compare_fusion.2
  10.1 0.1 and.30
  10.2 0.1 copy.71
  10.3 0.8 select_reduce_fusion.1
  11.1 0.1 iota_add_fusion
  11.2 0.1 add.43
  11.3 0.7 copy.75
  12.0 0.1 reduce-window.8
  12.1 0.1 reduce
  12.2 0.1 convert_reduce_fusion
  12.3 2.9 %slice_reduce_fusion = (bf16[256,256]{1,0:T(8,128)(2,1)}, bf16[256,256]{1,0:T(8,128)(2,1)}) fusion(bf16[256,2,256]{2,1,0:T(2,128)(2,1)} %param.13), kind=kLoop, calls=%fused_computation.33 | loop fusion | bytes 524288 | tf_op jit(solution)/shard_map/slice | solution.py:85
  15.2 75.4 %all-gather.2.cloned.1.call-done = bf16[8192,2,256]{2,1,0:T(2,128)(2,1)} async-done(((bf16[1024,2,256]{2,1,0:T(2,128)(2,1)}), bf16[8192,2,256]{2,1,0:T(2,128)(2,1)}) %all-gather.2.cloned.1.call-update) | async-done | bytes 8388624 | tf_op jit(solution)/shard_map/all_gather | solution.py:37
  90.6 8.0 %copy.104 = bf16[1024,8,2,256]{3,1,2,0:T(8,128)(2,1)} copy(bf16[1024,8,2,256]{3,2,1,0:T(2,128)(2,1)} %bitcast.58) | data formatting | bytes 16777216
  98.6 0.0 copy-done
  98.6 4.6 %convolution_convert_fusion.2 = bf16[128,512]{1,0:T(8,128)(2,1)S(1)} fusion(bf16[128,8192]{1,0:T(8,128)(2,1)S(1)} %copy-done, bf16[8192,512]{1,0:T(8,128)(2,1)} %bitcast.57), kind=kOutput, calls=%fused_computation.20 | convolution fusion | flops 1073807360 | bytes 10616832 | tf_op jit(solution)/shard_map/dot_general | solution.py:39
  103.3 0.1 reshape_reshape.3
  103.4 0.2 fusion
  103.6 0.5 broadcast.98
  104.1 0.8 reduce.5
  104.9 0.9 reshape.170
  105.8 6.4 %all-to-all-start = ((bf16[8,2,8192]{2,1,0:T(2,128)(2,1)}), bf16[8,2,8192]{2,1,0:T(2,128)(2,1)S(1)}, u32[]{:S(2)}, u32[]{:S(2)}) async-start(bf16[8,2,8192]{2,1,0:T(2,128)(2,1)} %reshape.170), calls=%async_computation | async-start | bytes 524288 | tf_op jit(solution)/shard_map/all_to_all | solution.py:46
  112.2 0.0 all-reduce.2.cloned.1.call-start
  112.2 1.5 copy.105
  113.7 0.1 broadcast_in_dim.66
  113.8 0.1 reshape.154
  113.8 0.1 broadcast_compare_fusion
  114.0 5.5 %all-to-all-done = bf16[8,2,8192]{2,1,0:T(2,128)(2,1)S(1)} async-done(((bf16[8,2,8192]{2,1,0:T(2,128)(2,1)}), bf16[8,2,8192]{2,1,0:T(2,128)(2,1)S(1)}, u32[]{:S(2)}, u32[]{:S(2)}) %all-to-all-start) | async-done | bytes 262176 | tf_op jit(solution)/shard_map/all_to_all | solution.py:46
  119.4 1.0 reshape.171
  120.4 2.1 convolution_convert_fusion
  122.5 1.1 reshape.153
  123.7 0.0 copy-start.4
  123.7 1.2 fusion.40
  124.8 1.7 copy.74
  126.6 1.7 copy.103
  128.3 3.8 %fusion.1 = (f32[256,2,8]{0,2,1:T(8,128)S(1)}, f32[2,256,256,8]{2,1,3,0:T(8,128)}) fusion(pred[256,256]{0,1:T(8,128)(4,1)S(1)} %broadcast_compare_fusion, bf16[256,2,128,1]{0,2,3,1:T(8,128)(2,1)} %bitcast.67, bf16[256,2,8,128]{3,2,1,0:T(8,128)(2,1)S(1)} %bitcast.61), kind=kOutput, calls=%fused_computation.5 | convolution fusion | flops 271577088 | bytes 5455872 | tf_op jit(solution)/shard_map/rgjd,cgd->rgjc/dot_general | solution.py:73
  132.1 22.2 %pmax.7 = f32[256,2,8]{0,2,1:T(8,128)S(1)} all-reduce(f32[256,2,8]{0,2,1:T(8,128)S(1)} %get-tuple-element.25), channel_id=1, replica_groups=mesh['groups'=1,'seq'=4,'tensor'=4,'section'=2] {'seq','section'}, use_global_device_ids=true, to_apply=%region_6.7 | all-reduce | flops 4096 | bytes 32768 | tf_op jit(solution)/shard_map/pmax | solution.py:106
  154.2 3.2 %fusion.4 = f32[256,2,8]{0,2,1:T(8,128)S(1)} fusion(f32[2,256,256,8]{2,1,3,0:T(8,128)} %get-tuple-element.26, f32[256,2,8]{0,2,1:T(8,128)S(1)} %get-tuple-element.25, pred[256,256]{0,1:T(8,128)(4,1)S(1)} %broadcast_compare_fusion), kind=kLoop, calls=%fused_computation.8 | loop fusion | flops 4190208 | bytes 4292608 | tf_op jit(solution)/shard_map/reduce_sum | solution.py:16
  157.4 0.0 copy-done.4
  157.5 0.6 fusion.39
  158.1 0.0 copy-done.1
  158.1 0.0 copy-done.5
  158.1 2.3 bitcast_multiply_fusion
  160.4 0.0 all-reduce.2.cloned.1.call-update
  160.4 0.5 iota_compare_fusion.4
  161.0 0.7 reshape_squeeze.14
  161.7 5.7 %select_reduce_fusion = (f32[64,4,2,8]{3,1,2,0:T(4,128)S(1)}, f32[64,4,2,8,4]{3,4,1,2,0:T(4,128)S(1)}) fusion(pred[4,4]{1,0:T(4,128)(4,1)} %iota_compare_fusion.4, bf16[64,4,2,8,128]{4,3,2,1,0:T(8,128)(2,1)S(1)} %bitcast.62, bf16[64,4,2,128,1]{3,2,1,0,4:T(2,128)(2,1)} %bitcast.69), kind=kOutput, calls=%fused_computation.25 | convolution fusion | flops 4239360 | bytes 1261584 | tf_op jit(solution)/shard_map/rtgjd,rsgd->rtgjs/dot_general | solution.py:87
  167.4 0.0 copy-start.2
  167.4 0.8 copy.82
  168.2 1.3 convolution_bitcast_fusion
  169.6 1.5 copy.85
  171.1 3.0 %copy.87 = f32[256,2,8,128]{0,3,2,1:T(8,128)} copy(f32[256,2,8,128]{3,2,1,0:T(8,128)} %bitcast.59) | data formatting | bytes 4194304 | tf_op jit(solution)/shard_map/reshape | solution.py:104
  174.1 1.0 fusion.18
  175.2 0.1 copy.89
  175.3 1.1 copy.83
  176.4 27.0 %psum.15 = f32[256,2,8]{0,2,1:T(8,128)S(1)} all-reduce(f32[256,2,8]{0,2,1:T(8,128)S(1)} %copy-done.8), channel_id=1, replica_groups=mesh['groups'=1,'seq'=4,'tensor'=4,'section'=2] {'seq','section'}, use_global_device_ids=true, to_apply=%region_10.11 | all-reduce | flops 4096 | bytes 32768 | tf_op jit(solution)/shard_map/psum | solution.py:108
  203.4 24.4 %all-reduce.2.cloned.1.call-done = f32[256,2,8,128]{0,3,2,1:T(8,128)} async-done(((f32[256,2,8,128]{0,3,2,1:T(8,128)}), f32[256,2,8,128]{0,3,2,1:T(8,128)}) %all-reduce.2.cloned.1.call-update) | async-done | bytes 2097168 | tf_op jit(solution)/shard_map/psum | solution.py:108
  227.8 2.7 %divide_convert_fusion = bf16[256,2,8,128]{0,3,2,1:T(8,128)(2,1)S(1)} fusion(f32[256,2,8,128]{0,3,2,1:T(8,128)} %copy.87, f32[256,2,8,128]{0,3,2,1:T(8,128)} %all-reduce.2.cloned.1.call-done, f32[256,2,8]{0,2,1:T(8,128)S(1)} %get-tuple-element.16, f32[256,2,8]{0,2,1:T(8,128)S(1)} %get-tuple-element.18, f32[256,2,8]{0,2,1:T(8,128)S(1)} %get-tuple-element.17), kind=kLoop, calls=%fused_computation.12 | loop fusion | flops 2621440 | bytes 5292032 | tf_op jit(solution)/shard_map/convert_element_type | solution.py:115
  230.5 1.4 copy.90
  (20 shorter events, 0.1 us)
Async XLA Ops:
  7.2 91.5 %copy-start = (bf16[128,8192]{1,0:T(8,128)(2,1)S(1)}, bf16[128,8192]{1,0:T(8,128)(2,1)}, u32[]{:S(2)}) copy-start(bf16[128,8192]{1,0:T(8,128)(2,1)} %param.7) | copy-start | bytes 6291460
  7.2 83.5 %all-gather.2.cloned.1.call-start = ((), (), s32[]{:S(2)}) async-start(), calls=%async_computation.1 | async-start | bytes 9437184 | tf_op jit(solution)/shard_map/all_gather | solution.py:37
  105.8 13.6 %all-to-all-start = ((bf16[8,2,8192]{2,1,0:T(2,128)(2,1)}), bf16[8,2,8192]{2,1,0:T(2,128)(2,1)S(1)}, u32[]{:S(2)}, u32[]{:S(2)}) async-start(bf16[8,2,8192]{2,1,0:T(2,128)(2,1)} %reshape.170), calls=%async_computation | async-start | bytes 524288 | tf_op jit(solution)/shard_map/all_to_all | solution.py:46
  112.2 115.6 %all-reduce.2.cloned.1.call-start = ((), (), s32[]{:S(2)}) async-start(), calls=%async_computation.2 | async-start | bytes 4194304 | tf_op jit(solution)/shard_map/psum | solution.py:108
  123.7 33.8 %copy-start.4 = (bf16[256,2,256]{2,1,0:T(2,128)(2,1)}, bf16[256,2,256]{2,1,0:T(2,128)(2,1)S(1)}, u32[]{:S(2)}) copy-start(bf16[256,2,256]{2,1,0:T(2,128)(2,1)S(1)} %reshape.153) | copy-start | bytes 786436
  154.2 3.8 %copy-start.1 = (f32[2,256,256,8]{2,1,3,0:T(8,128)S(1)}, f32[2,256,256,8]{2,1,3,0:T(8,128)}, u32[]{:S(2)}) copy-start(f32[2,256,256,8]{2,1,3,0:T(8,128)} %get-tuple-element.26) | copy-start | bytes 12582916
  154.2 3.8 %copy-start.5 = (bf16[256,1,256]{0,2,1:T(8,128)(2,1)S(1)}, bf16[256,1,256]{0,2,1:T(8,128)(2,1)}, u32[]{:S(2)}) copy-start(bf16[256,1,256]{0,2,1:T(8,128)(2,1)} %copy.74) | copy-start | bytes 393220
  158.1 2.9 %copy-start.7 = (bf16[256,256]{1,0:T(8,128)(2,1)S(1)}, bf16[256,256]{1,0:T(8,128)(2,1)}, u32[]{:S(2)}) copy-start(bf16[256,256]{1,0:T(8,128)(2,1)} %get-tuple-element.13) | copy-start | bytes 393220
  158.1 3.6 %copy-start.6 = (bf16[256,256]{1,0:T(8,128)(2,1)S(1)}, bf16[256,256]{1,0:T(8,128)(2,1)}, u32[]{:S(2)}) copy-start(bf16[256,256]{1,0:T(8,128)(2,1)} %get-tuple-element.12) | copy-start | bytes 393220
  167.4 3.7 %copy-start.2 = (f32[64,4,2,8,4]{3,4,1,2,0:T(4,128)}, f32[64,4,2,8,4]{3,4,1,2,0:T(4,128)S(1)}, u32[]{:S(2)}) copy-start(f32[64,4,2,8,4]{3,4,1,2,0:T(4,128)S(1)} %get-tuple-element.24) | copy-start | bytes 196612
  169.6 4.6 %copy-start.9 = (pred[4,4]{1,0:T(4,128)(4,1)S(1)}, pred[4,4]{1,0:T(4,128)(4,1)}, u32[]{:S(2)}) copy-start(pred[4,4]{1,0:T(4,128)(4,1)} %iota_compare_fusion.4) | copy-start | bytes 52
  171.1 5.3 %copy-start.8 = (f32[256,2,8]{0,2,1:T(8,128)S(1)}, f32[256,2,8]{0,2,1:T(8,128)}, u32[]{:S(2)}) copy-start(f32[256,2,8]{0,2,1:T(8,128)} %get-tuple-element.19) | copy-start | bytes 49156
  171.1 3.0 %copy-start.3 = (f32[64,4,2,8,4]{3,4,1,2,0:T(4,128)S(1)}, f32[64,4,2,8,4]{3,4,1,2,0:T(4,128)}, u32[]{:S(2)}) copy-start(f32[64,4,2,8,4]{3,4,1,2,0:T(4,128)} %copy-done.2) | copy-start | bytes 196612
Sparse Core Ops, SparseCore 0:
  9.6 80.9 all-gather.1
  160.6 67.1 all-reduce.1
where the time goes:
time: 243 us; the launch traced here: 239 us
  waiting for transfers between devices  106 us (44%)
  blocking collectives  49.2 us (20%)
  local copies, waits for them, and re-layouts  32 us (13%)
  matrix products  20.1 us (8%)
  between operations  14.2 us (6%)
  other arithmetic  10.8 us (4%)
  starting transfers between devices  6.45 us (3%)
    all_gather x1, waiting for transfers between devices, per_device(): lax.all_gather(kv_weight, ('seq', 'section'), axis=0, tiled=True)  75.4 us
    psum x1, blocking collectives, per_device(): lax.psum((total * group_factor, weighted * group_factor[..., None]), ('se...  27 us
    psum x1, waiting for transfers between devices, per_device(): lax.psum((total * group_factor, weighted * group_factor[..., None]), ('se...  24.4 us
    pmax x1, blocking collectives, per_device(): top = lax.pmax(highest, ('seq', 'section'))  22.2 us
    unnamed x26, local copies, waits for them, and re-layouts  14.5 us
    all_to_all x1, starting transfers between devices, per_device(): lax.all_to_all(outgoing, ('seq', 'section'), split_axis=0, concat_axis=0,...  6.41 us
    dot_general x1, matrix products, per_device(): jnp.einsum('rtgjd,rsgd->rtgjs', asked_fresh_rows, fresh_key_rows, preferr...  5.71 us
    all_to_all x1, waiting for transfers between devices, per_device(): lax.all_to_all(outgoing, ('seq', 'section'), split_axis=0, concat_axis=0,...  5.47 us
  transfers between devices with their start and end apart: 3, of which 3 were waited for; matrix products, arithmetic and copies ran while one was open for 10% of the time, Pallas kernels for 0%

commit v1 on v0

--- a/solution.py
+++ b/solution.py
@@ -1,6 +1,10 @@
+import functools
+
 import jax
 import jax.numpy as jnp
 from jax import lax
+from jax.experimental import pallas as pl
+from jax.experimental.pallas import tpu as pltpu
 from jax.sharding import PartitionSpec as P
 
 HEAD_SIZE = 128
@@ -118,6 +122,517 @@
     return (cache_local, attended)
 
 
+MESH = pl.DeviceIdType.MESH
+
+
+def project_kernel(
+    chips,
+    planes,
+    prompts,
+    weight,
+    fresh,
+    gathered,
+    mine,
+    theirs,
+    from_sibling,
+    summed,
+    reduced,
+    own_sem,
+    send_sem,
+    plane_send_sem,
+    sum_send_sem,
+    fresh_send_sem,
+    line_sem,
+    plane_sem,
+    sibling_sem,
+    reduce_sem,
+    fresh_sem,
+    fresh_sibling_sem,
+):
+    z = lax.axis_index("seq")
+    t = lax.axis_index("tensor")
+    c = lax.axis_index("section")
+    other = 1 - c
+    me = z * 2 + c
+    piece = prompts.shape[1]
+    depth = weight.shape[0]
+    half = weight.shape[1] // 2
+    rows = 2 * planes * piece
+
+    def at(seq, tensor, section):
+        return {"seq": seq, "tensor": tensor, "section": section}
+
+    def remote(src, dst, ssem, rsem, where):
+        return pltpu.make_async_remote_copy(
+            src_ref=src,
+            dst_ref=dst,
+            send_sem=ssem,
+            recv_sem=rsem,
+            device_id=where,
+            device_id_type=MESH,
+        )
+
+    barrier = pltpu.get_barrier_semaphore()
+    for d in range(1, chips):
+        for s in range(2):
+            pl.semaphore_signal(
+                barrier, inc=1, device_id=at(lax.rem(z + d, chips), t, s), device_id_type=MESH
+            )
+    for d in range(1, planes):
+        pl.semaphore_signal(
+            barrier, inc=1, device_id=at(z, lax.rem(t + d, planes), c), device_id_type=MESH
+        )
+    pl.semaphore_signal(barrier, inc=1, device_id=at(z, t, other), device_id_type=MESH)
+
+    def columns(k):
+        return pl.ds(pl.multiple_of(k * depth, depth), depth)
+
+    own = pltpu.make_async_copy(
+        prompts.at[:, :, columns(me)], gathered.at[pl.ds(me * planes, planes)], own_sem
+    )
+    own.start()
+    pl.semaphore_wait(barrier, 2 * (chips - 1) + planes)
+
+    sends = []
+    copy = remote(
+        prompts.at[:, :, columns(z * 2 + other)],
+        gathered.at[pl.ds(me * planes, planes)],
+        send_sem.at[0],
+        line_sem.at[me],
+        at(z, t, other),
+    )
+    copy.start()
+    sends.append(copy)
+    for d in range(1, chips):
+        zt = lax.rem(z + d, chips)
+        for s in range(2):
+            copy = remote(
+                prompts.at[t, :, columns(zt * 2 + s)],
+                gathered.at[me * planes + t],
+                send_sem.at[2 * d - 1 + s],
+                line_sem.at[me],
+                at(zt, t, s),
+            )
+            copy.start()
+            sends.append(copy)
+
+    def forward(d):
+        zs = lax.rem(z + chips - d, chips)
+        for s in range(2):
+            src = zs * 2 + s
+            slot = src * planes + t
+            remote(
+                gathered.at[slot],
+                gathered.at[slot],
+                send_sem.at[0],
+                line_sem.at[src],
+                at(z, t, other),
+            ).wait_recv()
+            for e in range(1, planes):
+                copy = remote(
+                    gathered.at[slot],
+                    gathered.at[slot],
+                    plane_send_sem.at[d - 1, s, e - 1],
+                    plane_sem.at[src, t],
+                    at(z, lax.rem(t + e, planes), c),
+                )
+                copy.start()
+                sends.append(copy)
+
+    def multiply(d):
+        zs = lax.rem(z + chips - d, chips)
+        if d == 0:
+            own.wait()
+            sibling = pl.ds((z * 2 + other) * planes, planes)
+            remote(
+                gathered.at[sibling],
+                gathered.at[sibling],
+                send_sem.at[0],
+                line_sem.at[z * 2 + other],
+                at(z, t, other),
+            ).wait_recv()
+        else:
+            for s in range(2):
+                src = zs * 2 + s
+                for e in range(1, planes):
+                    te = lax.rem(t + e, planes)
+                    slot = src * planes + te
+                    remote(
+                        gathered.at[slot],
+                        gathered.at[slot],
+                        send_sem.at[0],
+                        plane_sem.at[src, te],
+                        at(z, te, c),
+                    ).wait_recv()
+        left = gathered[pl.ds(zs * 2 * planes, 2 * planes)].reshape(rows, depth)
+        theirs[d] = jnp.dot(
+            left,
+            weight[:, pl.ds(pl.multiple_of(other * half, half), half)],
+            preferred_element_type=jnp.float32,
+        )
+        copy = remote(
+            theirs.at[d],
+            from_sibling.at[d],
+            sum_send_sem.at[0, d],
+            sibling_sem.at[d],
+            at(z, t, other),
+        )
+        copy.start()
+        sends.append(copy)
+        mine[d] = jnp.dot(
+            left,
+            weight[:, pl.ds(pl.multiple_of(c * half, half), half)],
+            preferred_element_type=jnp.float32,
+        )
+        return copy
+
+    def pass_on(d, copy):
+        zs = lax.rem(z + chips - d, chips)
+        copy.wait_recv()
+        if d == 0:
+            return
+        summed[d - 1] = mine[d] + from_sibling[d]
+        out = remote(
+            summed.at[d - 1],
+            reduced.at[d - 1],
+            sum_send_sem.at[1, d],
+            reduce_sem.at[d - 1],
+            at(zs, t, c),
+        )
+        out.start()
+        sends.append(out)
+        return out
+
+    outs = []
+    held = multiply(0)
+    for d in range(1, chips):
+        forward(d)
+        if d == 1:
+            pass_on(0, held)
+        else:
+            later = multiply(d - 1)
+            outs.append(pass_on(d - 1, later))
+    held = multiply(chips - 1)
+    outs.append(pass_on(chips - 1, held))
+
+    total = mine[0] + from_sibling[0]
+    for d in range(1, chips):
+        outs[d - 1].wait_recv()
+        total = total + reduced[d - 1]
+    block = pl.ds(pl.multiple_of(z * rows, rows), rows)
+    fresh[c, block] = total.astype(jnp.bfloat16)
+    for d in range(1, chips):
+        copy = remote(
+            fresh.at[c, block],
+            fresh.at[c, block],
+            fresh_send_sem.at[0, d],
+            fresh_sem.at[z],
+            at(lax.rem(z + d, chips), t, c),
+        )
+        copy.start()
+        sends.append(copy)
+    for d in range(chips):
+        zs = lax.rem(z + chips - d, chips)
+        arrived = pl.ds(pl.multiple_of(zs * rows, rows), rows)
+        if d > 0:
+            remote(
+                fresh.at[c, arrived],
+                fresh.at[c, arrived],
+                send_sem.at[0],
+                fresh_sem.at[zs],
+                at(z, t, other),
+            ).wait_recv()
+        copy = remote(
+            fresh.at[c, arrived],
+            fresh.at[c, arrived],
+            fresh_send_sem.at[1, d],
+            fresh_sibling_sem.at[zs],
+            at(z, t, other),
+        )
+        copy.start()
+        sends.append(copy)
+    for d in range(chips):
+        zs = lax.rem(z + chips - d, chips)
+        arrived = pl.ds(pl.multiple_of(zs * rows, rows), rows)
+        remote(
+            fresh.at[other, arrived],
+            fresh.at[other, arrived],
+            send_sem.at[0],
+            fresh_sibling_sem.at[zs],
+            at(z, t, other),
+        ).wait_recv()
+    for copy in sends:
+        copy.wait_send()
+
+
+def project(prompts, weight, chips, planes):
+    tok_rows, width = prompts.shape
+    depth = weight.shape[0]
+    half = weight.shape[1] // 2
+    piece = tok_rows // planes
+    rows = 2 * tok_rows
+    shards = 2 * chips
+    f32 = jnp.float32
+    dma = pltpu.SemaphoreType.DMA
+    return pl.pallas_call(
+        functools.partial(project_kernel, chips, planes),
+        out_shape=jax.ShapeDtypeStruct((2, chips * rows, half), jnp.bfloat16),
+        in_specs=[
+            pl.BlockSpec(memory_space=pl.ANY),
+            pl.BlockSpec(memory_space=pltpu.VMEM),
+        ],
+        out_specs=pl.BlockSpec(memory_space=pltpu.VMEM),
+        scratch_shapes=[
+            pltpu.VMEM((shards * planes, piece, depth), jnp.bfloat16),
+            pltpu.VMEM((chips, rows, half), f32),
+            pltpu.VMEM((chips, rows, half), f32),
+            pltpu.VMEM((chips, rows, half), f32),
+            pltpu.VMEM((chips - 1, rows, half), f32),
+            pltpu.VMEM((chips - 1, rows, half), f32),
+            dma,
+            dma((2 * chips - 1,)),
+            dma((chips - 1, 2, planes - 1)),
+            dma((2, chips)),
+            dma((2, chips)),
+            dma((shards,)),
+            dma((shards, planes)),
+            dma((chips,)),
+            dma((chips - 1,)),
+            dma((chips,)),
+            dma((chips,)),
+        ],
+        compiler_params=pltpu.CompilerParams(
+            collective_id=0, has_side_effects=True, vmem_limit_bytes=40 * 2**20
+        ),
+        name="project",
+    )(prompts.reshape(planes, piece, width), weight)
+
+
+TILE_REQUESTS = 8
+TOKEN_BLOCK = 128
+
+
+def attend_kernel(
+    piece,
+    lengths,
+    piece_owner,
+    piece_slot,
+    fresh,
+    queries,
+    decode,
+    cache,
+    attended,
+    ends,
+    source,
+    score,
+    owner_max,
+    weighted,
+):
+    owners = owner_max.shape[1]
+    requests = lengths.shape[0]
+    pieces = piece_owner.shape[0]
+    tile_rows = TILE_REQUESTS * DECODE_STEPS
+    kv_heads = fresh.shape[2] // HEAD_SIZE
+    local = fresh.shape[2]
+    group = queries.shape[1] // (kv_heads * HEAD_SIZE)
+    lanes = group * tile_rows
+    per_block = TOKEN_BLOCK // piece
+    scale = HEAD_SIZE ** (-0.5)
+    me = lax.axis_index("seq") * lax.axis_size("section") + lax.axis_index("section")
+
+    ends[0] = 0
+
+    def add_length(r, total):
+        total = total + lengths[r]
+        ends[r + 1] = total
+        return total
+
+    lax.fori_loop(0, requests, add_length, jnp.int32(0))
+
+    slots = source.shape[0]
+    for j in range(slots):
+        source[j] = -1
+
+    def place(p, carry):
+        @pl.when(piece_owner[p] == me)
+        def _():
+            source[piece_slot[p]] = p
+
+        return carry
+
+    lax.fori_loop(0, pieces, place, 0)
+    for j in range(slots):
+        p = source[j]
+        into = pl.ds(j * piece, piece)
+
+        @pl.when(p >= 0)
+        def _():
+            rows = pl.ds(pl.multiple_of(p * piece, piece), piece)
+            cache[into, :local] = fresh[0, rows]
+            cache[into, local:] = fresh[1, rows]
+
+        @pl.when(p < 0)
+        def _():
+            cache[into] = jnp.zeros((piece, 2 * local), cache.dtype)
+
+    f32, bf16 = jnp.float32, jnp.bfloat16
+    lane_row = lax.broadcasted_iota(jnp.int32, (1, lanes), 1) % tile_rows
+    lane_request = lane_row // DECODE_STEPS
+    token = lax.broadcasted_iota(jnp.int32, (TOKEN_BLOCK, lanes), 0)
+    new_row = lax.broadcasted_iota(jnp.int32, (tile_rows, lanes), 0)
+    new_mask = (new_row // DECODE_STEPS == lane_request) & (new_row <= lane_row)
+
+    def outer(a, b):
+        return lax.dot_general(a, b, (((1,), (1,)), ((), ())), preferred_element_type=f32)
+
+    def inner(a, b):
+        return lax.dot_general(a, b, (((0,), (0,)), ((), ())), preferred_element_type=f32)
+
+    def tile(i, carry):
+        first = i * TILE_REQUESTS
+        begin = jnp.zeros((1, lanes), jnp.int32)
+        end = jnp.zeros((1, lanes), jnp.int32)
+        for r in range(TILE_REQUESTS):
+            begin = jnp.where(lane_request == r, ends[first + r], begin)
+            end = jnp.where(lane_request == r, ends[first + r + 1], end)
+        low = ends[first] // TOKEN_BLOCK
+        high = (ends[first + TILE_REQUESTS] + TOKEN_BLOCK - 1) // TOKEN_BLOCK
+        rows = pl.ds(pl.multiple_of(i * tile_rows, tile_rows), tile_rows)
+        asked = []
+        for g in range(kv_heads):
+            asked.append(
+                jnp.concatenate(
+                    [
+                        queries[rows, (g * group + j) * HEAD_SIZE : (g * group + j + 1) * HEAD_SIZE]
+                        for j in range(group)
+                    ],
+                    axis=0,
+                )
+            )
+        owner_max[...] = jnp.full(owner_max.shape, masked_value, f32)
+
+        def mask_of(b):
+            place = token + b * TOKEN_BLOCK
+            return (place >= begin) & (place < end)
+
+        def scores(b, carry):
+            allowed = mask_of(b)
+            span = pl.ds(pl.multiple_of(b * TOKEN_BLOCK, TOKEN_BLOCK), TOKEN_BLOCK)
+            for g in range(kv_heads):
+                head = slice(g * HEAD_SIZE, (g + 1) * HEAD_SIZE)
+                s = jnp.where(allowed, outer(fresh[0, span, head], asked[g]) * scale, masked_value)
+                score[g, span] = s
+                tops = jnp.max(s.reshape(per_block, piece, lanes), axis=1)
+                for q in range(per_block):
+                    o = pl.ds(piece_owner[b * per_block + q], 1)
+                    owner_max[g, o] = jnp.maximum(owner_max[g, o], tops[q : q + 1])
+            return carry
+
+        lax.fori_loop(low, high, scores, 0)
+
+        tops = []
+        starts = []
+        for g in range(kv_heads):
+            keys = decode[rows, g * HEAD_SIZE : (g + 1) * HEAD_SIZE]
+            values = decode[rows, local + g * HEAD_SIZE : local + (g + 1) * HEAD_SIZE]
+            s = jnp.where(new_mask, outer(keys, asked[g]) * scale, masked_value)
+            new_top = jnp.max(s, axis=0, keepdims=True)
+            p = jnp.where(new_mask, jnp.exp(s - new_top), 0.0)
+            top = jnp.maximum(new_top, jnp.max(owner_max[g], axis=0, keepdims=True))
+            factor = jnp.exp(new_top - top)
+            weighted[g] = inner(values, p.astype(bf16)) * factor
+            tops.append(top)
+            starts.append(jnp.sum(p, axis=0, keepdims=True) * factor)
+
+        def weigh(b, totals):
+            allowed = mask_of(b)
+            span = pl.ds(pl.multiple_of(b * TOKEN_BLOCK, TOKEN_BLOCK), TOKEN_BLOCK)
+            results = []
+            for g in range(kv_heads):
+                head = slice(g * HEAD_SIZE, (g + 1) * HEAD_SIZE)
+                highest = jnp.concatenate(
+                    [
+                        jnp.broadcast_to(
+                            owner_max[g, pl.ds(piece_owner[b * per_block + q], 1)], (piece, lanes)
+                        )
+                        for q in range(per_block)
+                    ],
+                    axis=0,
+                )
+                factor = jnp.exp(highest - tops[g])
+                p = jnp.where(allowed, jnp.exp(score[g, span] - highest), 0.0)
+                w = p.astype(bf16).astype(f32) * factor
+                upper = w.astype(bf16)
+                lower = (w - upper.astype(f32)).astype(bf16)
+                values = fresh[1, span, head]
+                weighted[g] += inner(values, upper) + inner(values, lower)
+                results.append(totals[g] + jnp.sum(p * factor, axis=0, keepdims=True))
+            return tuple(results)
+
+        totals = lax.fori_loop(low, high, weigh, tuple(starts))
+        for g in range(kv_heads):
+            result = (weighted[g] / totals[g]).T.astype(bf16)
+            for j in range(group):
+                attended[rows, (g * group + j) * HEAD_SIZE : (g * group + j + 1) * HEAD_SIZE] = result[
+                    j * tile_rows : (j + 1) * tile_rows
+                ]
+        return carry
+
+    lax.fori_loop(0, requests // TILE_REQUESTS, tile, 0)
+
+
+def attend(lengths, piece_owner, piece_slot, fresh, queries, decode, shards):
+    tokens = fresh.shape[1]
+    local = fresh.shape[2]
+    piece = tokens // piece_owner.shape[0]
+    slots = shards
+    kv_heads = local // HEAD_SIZE
+    group = queries.shape[1] // local
+    lanes = group * TILE_REQUESTS * DECODE_STEPS
+    smem = pl.BlockSpec(memory_space=pltpu.SMEM)
+    vmem = pl.BlockSpec(memory_space=pltpu.VMEM)
+    return pl.pallas_call(
+        functools.partial(attend_kernel, piece),
+        out_shape=(
+            jax.ShapeDtypeStruct((slots * piece, 2 * local), jnp.bfloat16),
+            jax.ShapeDtypeStruct(queries.shape, jnp.bfloat16),
+        ),
+        in_specs=[smem, smem, smem, vmem, vmem, vmem],
+        out_specs=(vmem, vmem),
+        scratch_shapes=[
+            pltpu.SMEM((lengths.shape[0] + 1,), jnp.int32),
+            pltpu.SMEM((slots,), jnp.int32),
+            pltpu.VMEM((kv_heads, tokens, lanes), jnp.float32),
+            pltpu.VMEM((kv_heads, shards, lanes), jnp.float32),
+            pltpu.VMEM((kv_heads, HEAD_SIZE, lanes), jnp.float32),
+        ],
+        compiler_params=pltpu.CompilerParams(vmem_limit_bytes=32 * 2**20),
+        name="attend",
+    )(lengths, piece_owner, piece_slot, fresh, queries, decode)
+
+
+def per_device_fused(
+    mesh, prompts, kv_weight, lengths, piece_owner, piece_slot, queries, decode_key_value
+):
+    chips, planes = mesh.shape["seq"], mesh.shape["tensor"]
+    depth, _, local = kv_weight.shape
+    fresh = project(prompts, kv_weight.reshape(depth, 2 * local), chips, planes)
+    cache, attended = attend(
+        lengths,
+        piece_owner,
+        piece_slot,
+        fresh,
+        queries,
+        decode_key_value.reshape(-1, 2 * local),
+        2 * chips,
+    )
+    return cache.reshape(-1, 2, local), attended
+
+
+def fits(mesh):
+    return mesh.shape["section"] == 2 and mesh.shape["seq"] <= 4
+
+
 def solution(mesh):
     placed = (
         P(("groups", "seq", "section"), None),
@@ -129,7 +644,7 @@
         P("groups", None, "tensor"),
     )
     return jax.shard_map(
-        per_device,
+        functools.partial(per_device_fused, mesh) if fits(mesh) else per_device,
         mesh=mesh,
         in_specs=placed,
         out_specs=(P(("groups", "seq", "section"), None, "tensor"), P("groups", "tensor")),

time: 243 us -> 77.4 us (0.32); the launches traced: 239 us -> 77.3 us
  waiting for transfers between devices: 106 us -> 0 us
  Pallas kernels: 0 us -> 73.2 us
  blocking collectives: 49.2 us -> 0 us
  local copies, waits for them, and re-layouts: 32 us -> 3.37 us
  matrix products: 20.1 us -> 0 us
  between operations: 14.2 us -> 0.73 us
  other arithmetic: 10.8 us -> 0 us
  starting transfers between devices: 6.45 us -> 0 us
    all_gather x1 -> x0, waiting for transfers between devices: 75.4 us -> none  [per_device(): lax.all_gather(kv_weight, ('seq', 'section'), axis=0, tiled=True)]
    pallas_call x0 -> x2, Pallas kernels: none -> 73.2 us  [the longest x1 57.2 us: project(): pl.pallas_call(functools.partial(project_kernel, chips, planes), out_shap...]
    psum x1 -> x0, blocking collectives: 27 us -> none  [per_device(): lax.psum((total * group_factor, weighted * group_factor[..., None]), ('se...]
    psum x1 -> x0, waiting for transfers between devices: 24.4 us -> none  [per_device(): lax.psum((total * group_factor, weighted * group_factor[..., None]), ('se...]
    pmax x1 -> x0, blocking collectives: 22.2 us -> none  [per_device(): top = lax.pmax(highest, ('seq', 'section'))]
    dot_general x7 -> x0, matrix products: 20.1 us -> none  [the longest x1 5.71 us: per_device(): jnp.einsum('rtgjd,rsgd->rtgjs', asked_fresh_rows, fresh_key_rows, preferr...]
    unnamed x26 -> x12, local copies, waits for them, and re-layouts: 14.5 us -> 2.61 us
    all_to_all x1 -> x0, starting transfers between devices: 6.41 us -> none  [per_device(): lax.all_to_all(outgoing, ('seq', 'section'), split_axis=0, concat_axis=0,...]
  transfers between devices with their start and end apart: 3 -> 0, of which waited for: 3 -> 0; matrix products, arithmetic and copies ran while one was open for 10% -> 0% of each run, Pallas kernels for 0% -> 0%
where the time goes in v1:
time: 77.4 us; the launch traced here: 77.3 us
  Pallas kernels  73.2 us (95%)
  local copies, waits for them, and re-layouts  3.37 us (4%)
    pallas_call x1, Pallas kernels, project(): pl.pallas_call(functools.partial(project_kernel, chips, planes), out_shap...  57.2 us
    pallas_call x1, Pallas kernels, attend(): pl.pallas_call(functools.partial(attend_kernel, piece), out_shape=(jax.Sh...  15.9 us
    unnamed x12, local copies, waits for them, and re-layouts  2.61 us

profile of v1, /device:TPU:9, one launch (start us, length us, event | category | flops | bytes accessed | tf_op | source)
XLA Modules:
  0.0 77.3 jit_solution(1538257699094613014)
XLA Ops:
  0.6 0.0 copy-start
  0.6 1.1 %copy.10 = bf16[32,8,2,256]{3,1,2,0:T(8,128)(2,1)S(1)} copy(bf16[32,8,2,256]{3,2,1,0:T(2,128)(2,1)} %bitcast.9) | data formatting | bytes 524288
  1.8 1.4 %copy.9 = bf16[128,8,2,256]{3,1,2,0:T(8,128)(2,1)S(1)} copy(bf16[128,8,2,256]{3,2,1,0:T(2,128)(2,1)} %bitcast.8) | data formatting | bytes 2097152
  3.2 0.0 copy-done
  3.2 0.0 copy-start.1
  3.2 0.0 copy-start.2
  3.3 0.0 copy-start.3
  3.3 0.0 copy-start.4
  3.3 57.2 %project.1.fresh = bf16[2,1024,256]{2,1,0:T(8,128)(2,1)S(1)} custom-call(bf16[4,32,8192]{2,1,0:T(8,128)(2,1)S(1)} %bitcast.6, bf16[1024,512]{1,0:T(8,128)(2,1)S(1)} %bitcast.5), custom_call_target="tpu_custom_call" | custom-call | tf_op jit(solution)/shard_map/project/pallas_call | solution.py:377
  60.5 0.0 copy-done.1
  60.5 0.0 copy-done.2
  60.6 0.0 copy-done.3
  60.6 0.0 copy-done.4
  60.6 15.9 %attend.1 = (bf16[256,512]{1,0:T(8,128)(2,1)S(1)}, bf16[256,2048]{1,0:T(8,128)(2,1)}) custom-call(s32[64]{0:T(128)S(1)} %copy-done.2, s32[32]{0:T(128)S(1)} %copy-done.3, s32[32]{0:T(128)S(1)} %copy-done.4, bf16[2,1024,256]{2,1,0:T(8,128)(2,1)S(1)} %project.1.fresh, bf16[256,2048]{1,0:T(8,128)(2,1)S(1)} %copy-done.1, bf16[256,512]{1,0:T(8,128)(2,1)S(1)} %bitcast.7), custom_call_target="tpu_custom_call" | custom-call | tf_op jit(solution)/shard_map/attend/pallas_call | solution.py:594
  76.5 0.8 reshape.19
Async XLA Ops:
  0.6 2.6 %copy-start = (bf16[128,8192]{1,0:T(8,128)(2,1)S(1)}, bf16[128,8192]{1,0:T(8,128)(2,1)}, u32[]{:S(2)}) copy-start(bf16[128,8192]{1,0:T(8,128)(2,1)} %param.7) | copy-start | bytes 6291460
  3.2 57.3 %copy-start.1 = (bf16[256,2048]{1,0:T(8,128)(2,1)S(1)}, bf16[256,2048]{1,0:T(8,128)(2,1)}, u32[]{:S(2)}) copy-start(bf16[256,2048]{1,0:T(8,128)(2,1)} %queries.1) | copy-start | bytes 3145732
  3.2 57.3 %copy-start.2 = (s32[64]{0:T(128)S(1)}, s32[64]{0:T(128)}, u32[]{:S(2)}) copy-start(s32[64]{0:T(128)} %lengths.1) | copy-start | bytes 772
  3.3 57.3 %copy-start.3 = (s32[32]{0:T(128)S(1)}, s32[32]{0:T(128)}, u32[]{:S(2)}) copy-start(s32[32]{0:T(128)} %piece_owner.1) | copy-start | bytes 388
  3.3 57.3 %copy-start.4 = (s32[32]{0:T(128)S(1)}, s32[32]{0:T(128)}, u32[]{:S(2)}) copy-start(s32[32]{0:T(128)} %piece_slot.1) | copy-start | bytes 388

commit v2 on v1

--- a/solution.py
+++ b/solution.py
@@ -409,11 +409,12 @@
 
 
 TILE_REQUESTS = 8
-TOKEN_BLOCK = 128
+TOKEN_BLOCK = 256
 
 
 def attend_kernel(
     piece,
+    owners,
     lengths,
     piece_owner,
     piece_slot,
@@ -425,10 +426,12 @@
     ends,
     source,
     score,
-    owner_max,
+    piece_top,
+    piece_factor,
+    owner_of,
+    values_across,
     weighted,
 ):
-    owners = owner_max.shape[1]
     requests = lengths.shape[0]
     pieces = piece_owner.shape[0]
     tile_rows = TILE_REQUESTS * DECODE_STEPS
@@ -468,14 +471,23 @@
         @pl.when(p >= 0)
         def _():
             rows = pl.ds(pl.multiple_of(p * piece, piece), piece)
-            cache[into, :local] = fresh[0, rows]
-            cache[into, local:] = fresh[1, rows]
+            cache[into, 0] = fresh[0, rows]
+            cache[into, 1] = fresh[1, rows]
 
         @pl.when(p < 0)
         def _():
-            cache[into] = jnp.zeros((piece, 2 * local), cache.dtype)
+            cache[into] = jnp.zeros((piece, 2, local), cache.dtype)
 
     f32, bf16 = jnp.float32, jnp.bfloat16
+    blocks = owner_of.shape[0]
+    for b in range(blocks):
+        for q in range(per_block):
+            owner_of[b, q : q + 1] = jnp.full((1, lanes), piece_owner[b * per_block + q], jnp.int32)
+        span = slice(b * TOKEN_BLOCK, (b + 1) * TOKEN_BLOCK)
+        for g in range(kv_heads):
+            turned = fresh[1, span, g * HEAD_SIZE : (g + 1) * HEAD_SIZE].T
+            values_across[g, b, :, :TOKEN_BLOCK] = turned
+            values_across[g, b, :, TOKEN_BLOCK:] = turned
     lane_row = lax.broadcasted_iota(jnp.int32, (1, lanes), 1) % tile_rows
     lane_request = lane_row // DECODE_STEPS
     token = lax.broadcasted_iota(jnp.int32, (TOKEN_BLOCK, lanes), 0)
@@ -509,64 +521,58 @@
                     axis=0,
                 )
             )
-        owner_max[...] = jnp.full(owner_max.shape, masked_value, f32)
-
-        def mask_of(b):
-            place = token + b * TOKEN_BLOCK
-            return (place >= begin) & (place < end)
+        piece_top[...] = jnp.full(piece_top.shape, masked_value, f32)
 
         def scores(b, carry):
-            allowed = mask_of(b)
+            where = token + b * TOKEN_BLOCK
+            allowed = (where >= begin) & (where < end)
             span = pl.ds(pl.multiple_of(b * TOKEN_BLOCK, TOKEN_BLOCK), TOKEN_BLOCK)
             for g in range(kv_heads):
                 head = slice(g * HEAD_SIZE, (g + 1) * HEAD_SIZE)
                 s = jnp.where(allowed, outer(fresh[0, span, head], asked[g]) * scale, masked_value)
                 score[g, span] = s
-                tops = jnp.max(s.reshape(per_block, piece, lanes), axis=1)
-                for q in range(per_block):
-                    o = pl.ds(piece_owner[b * per_block + q], 1)
-                    owner_max[g, o] = jnp.maximum(owner_max[g, o], tops[q : q + 1])
+                piece_top[g, b] = jnp.max(s.reshape(per_block, piece, lanes), axis=1)
             return carry
 
         lax.fori_loop(low, high, scores, 0)
 
-        tops = []
         starts = []
         for g in range(kv_heads):
-            keys = decode[rows, g * HEAD_SIZE : (g + 1) * HEAD_SIZE]
-            values = decode[rows, local + g * HEAD_SIZE : local + (g + 1) * HEAD_SIZE]
+            keys = decode[rows, 0, g * HEAD_SIZE : (g + 1) * HEAD_SIZE]
+            values = decode[rows, 1, g * HEAD_SIZE : (g + 1) * HEAD_SIZE]
             s = jnp.where(new_mask, outer(keys, asked[g]) * scale, masked_value)
             new_top = jnp.max(s, axis=0, keepdims=True)
             p = jnp.where(new_mask, jnp.exp(s - new_top), 0.0)
-            top = jnp.maximum(new_top, jnp.max(owner_max[g], axis=0, keepdims=True))
+            highest = piece_top[g]
+            top = jnp.maximum(new_top, jnp.max(highest, axis=(0, 1))[None, :])
+            for o in range(owners):
+                mine = owner_of[...] == o
+                most = jnp.max(jnp.where(mine, highest, masked_value), axis=(0, 1))
+                highest = jnp.where(mine, most[None, None, :], highest)
+            piece_top[g] = highest
+            piece_factor[g] = jnp.exp(highest - top[None])
             factor = jnp.exp(new_top - top)
             weighted[g] = inner(values, p.astype(bf16)) * factor
-            tops.append(top)
             starts.append(jnp.sum(p, axis=0, keepdims=True) * factor)
 
         def weigh(b, totals):
-            allowed = mask_of(b)
             span = pl.ds(pl.multiple_of(b * TOKEN_BLOCK, TOKEN_BLOCK), TOKEN_BLOCK)
             results = []
             for g in range(kv_heads):
-                head = slice(g * HEAD_SIZE, (g + 1) * HEAD_SIZE)
-                highest = jnp.concatenate(
-                    [
-                        jnp.broadcast_to(
-                            owner_max[g, pl.ds(piece_owner[b * per_block + q], 1)], (piece, lanes)
-                        )
-                        for q in range(per_block)
-                    ],
-                    axis=0,
-                )
-                factor = jnp.exp(highest - tops[g])
-                p = jnp.where(allowed, jnp.exp(score[g, span] - highest), 0.0)
-                w = p.astype(bf16).astype(f32) * factor
+                s = score[g, span].reshape(per_block, piece, lanes)
+                factor = piece_factor[g, b]
+                p = jnp.exp(s - piece_top[g, b][:, None, :])
+                w = p.astype(bf16).astype(f32) * factor[:, None, :]
+                w = w.reshape(TOKEN_BLOCK, lanes)
                 upper = w.astype(bf16)
                 lower = (w - upper.astype(f32)).astype(bf16)
-                values = fresh[1, span, head]
-                weighted[g] += inner(values, upper) + inner(values, lower)
-                results.append(totals[g] + jnp.sum(p * factor, axis=0, keepdims=True))
+                weighted[g] += jnp.dot(
+                    values_across[g, b],
+                    jnp.concatenate([upper, lower], axis=0),
+                    preferred_element_type=f32,
+                )
+                sums = jnp.sum(p, axis=1) * factor
+                results.append(totals[g] + jnp.sum(sums, axis=0, keepdims=True))
             return tuple(results)
 
         totals = lax.fori_loop(low, high, weigh, tuple(starts))
@@ -586,15 +592,16 @@
     local = fresh.shape[2]
     piece = tokens // piece_owner.shape[0]
     slots = shards
+    blocks = tokens // TOKEN_BLOCK
     kv_heads = local // HEAD_SIZE
     group = queries.shape[1] // local
     lanes = group * TILE_REQUESTS * DECODE_STEPS
     smem = pl.BlockSpec(memory_space=pltpu.SMEM)
     vmem = pl.BlockSpec(memory_space=pltpu.VMEM)
     return pl.pallas_call(
-        functools.partial(attend_kernel, piece),
+        functools.partial(attend_kernel, piece, shards),
         out_shape=(
-            jax.ShapeDtypeStruct((slots * piece, 2 * local), jnp.bfloat16),
+            jax.ShapeDtypeStruct((slots * piece, 2, local), jnp.bfloat16),
             jax.ShapeDtypeStruct(queries.shape, jnp.bfloat16),
         ),
         in_specs=[smem, smem, smem, vmem, vmem, vmem],
@@ -603,7 +610,10 @@
             pltpu.SMEM((lengths.shape[0] + 1,), jnp.int32),
             pltpu.SMEM((slots,), jnp.int32),
             pltpu.VMEM((kv_heads, tokens, lanes), jnp.float32),
-            pltpu.VMEM((kv_heads, shards, lanes), jnp.float32),
+            pltpu.VMEM((kv_heads, blocks, TOKEN_BLOCK // piece, lanes), jnp.float32),
+            pltpu.VMEM((kv_heads, blocks, TOKEN_BLOCK // piece, lanes), jnp.float32),
+            pltpu.VMEM((blocks, TOKEN_BLOCK // piece, lanes), jnp.int32),
+            pltpu.VMEM((kv_heads, blocks, HEAD_SIZE, 2 * TOKEN_BLOCK), jnp.bfloat16),
             pltpu.VMEM((kv_heads, HEAD_SIZE, lanes), jnp.float32),
         ],
         compiler_params=pltpu.CompilerParams(vmem_limit_bytes=32 * 2**20),
@@ -623,14 +633,14 @@
         piece_slot,
         fresh,
         queries,
-        decode_key_value.reshape(-1, 2 * local),
+        decode_key_value,
         2 * chips,
     )
-    return cache.reshape(-1, 2, local), attended
+    return cache, attended
 
 
 def fits(mesh):
-    return mesh.shape["section"] == 2 and mesh.shape["seq"] <= 4
+    return mesh.shape["groups"] == 1 and mesh.shape["section"] == 2 and mesh.shape["seq"] <= 4
 
 
 def solution(mesh):

time: 77.4 us -> 75.4 us (0.974)
  local copies, waits for them, and re-layouts: 3.37 us -> 1.91 us
    unnamed x12 -> x13, local copies, waits for them, and re-layouts: 2.61 us -> 1.91 us
where the time goes in v2:
time: 75.4 us; the launch traced here: 75.2 us
  Pallas kernels  72.6 us (96%)
  local copies, waits for them, and re-layouts  1.91 us (3%)
    pallas_call x1, Pallas kernels, project(): pl.pallas_call(functools.partial(project_kernel, chips, planes), out_shap...  57.2 us
    pallas_call x1, Pallas kernels, attend(): pl.pallas_call(functools.partial(attend_kernel, piece, shards), out_shape...  15.4 us
    unnamed x13, local copies, waits for them, and re-layouts  1.91 us

profile of v2, /device:TPU:9, one launch (start us, length us, event | category | flops | bytes accessed | tf_op | source)
XLA Modules:
  0.0 75.2 jit_solution(2218374206190692959)
XLA Ops:
  0.6 0.0 copy-start
  0.6 1.6 %copy.9 = bf16[128,8,2,256]{3,1,2,0:T(8,128)(2,1)S(1)} copy(bf16[128,8,2,256]{3,2,1,0:T(2,128)(2,1)} %bitcast.5) | data formatting | bytes 2097152
  2.2 0.3 copy-done
  2.5 0.0 copy-start.1
  2.5 0.0 copy-start.2
  2.5 0.0 copy-start.3
  2.5 0.0 copy-start.4
  2.5 0.0 copy-start.5
  2.6 57.2 %project.1.fresh = bf16[2,1024,256]{2,1,0:T(8,128)(2,1)S(1)} custom-call(bf16[4,32,8192]{2,1,0:T(8,128)(2,1)S(1)} %bitcast.4, bf16[1024,512]{1,0:T(8,128)(2,1)S(1)} %bitcast.3), custom_call_target="tpu_custom_call" | custom-call | tf_op jit(solution)/shard_map/project/pallas_call | solution.py:377
  59.8 0.0 copy-done.1
  59.8 0.0 copy-done.2
  59.8 0.0 copy-done.3
  59.8 0.0 copy-done.4
  59.8 0.0 copy-done.5
  59.9 15.4 %attend.1 = (bf16[256,2,256]{2,1,0:T(2,128)(2,1)}, bf16[256,2048]{1,0:T(8,128)(2,1)}) custom-call(s32[64]{0:T(128)S(1)} %copy-done.3, s32[32]{0:T(128)S(1)} %copy-done.4, s32[32]{0:T(128)S(1)} %copy-done.5, bf16[2,1024,256]{2,1,0:T(8,128)(2,1)S(1)} %project.1.fresh, bf16[256,2048]{1,0:T(8,128)(2,1)S(1)} %copy-done.1, bf16[256,2,256]{2,1,0:T(2,128)(2,1)S(1)} %copy-done.2), custom_call_target="tpu_custom_call" | custom-call | tf_op jit(solution)/shard_map/attend/pallas_call | solution.py:601
Async XLA Ops:
  0.6 1.9 %copy-start = (bf16[128,8192]{1,0:T(8,128)(2,1)S(1)}, bf16[128,8192]{1,0:T(8,128)(2,1)}, u32[]{:S(2)}) copy-start(bf16[128,8192]{1,0:T(8,128)(2,1)} %param.7) | copy-start | bytes 6291460
  2.5 57.3 %copy-start.1 = (bf16[256,2048]{1,0:T(8,128)(2,1)S(1)}, bf16[256,2048]{1,0:T(8,128)(2,1)}, u32[]{:S(2)}) copy-start(bf16[256,2048]{1,0:T(8,128)(2,1)} %queries.1) | copy-start | bytes 3145732
  2.5 57.3 %copy-start.2 = (bf16[256,2,256]{2,1,0:T(2,128)(2,1)S(1)}, bf16[256,2,256]{2,1,0:T(2,128)(2,1)}, u32[]{:S(2)}) copy-start(bf16[256,2,256]{2,1,0:T(2,128)(2,1)} %decode.1) | copy-start | bytes 786436
  2.5 57.3 %copy-start.3 = (s32[64]{0:T(128)S(1)}, s32[64]{0:T(128)}, u32[]{:S(2)}) copy-start(s32[64]{0:T(128)} %lengths.1) | copy-start | bytes 772
  2.5 57.3 %copy-start.4 = (s32[32]{0:T(128)S(1)}, s32[32]{0:T(128)}, u32[]{:S(2)}) copy-start(s32[32]{0:T(128)} %piece_owner.1) | copy-start | bytes 388
  2.5 57.3 %copy-start.5 = (s32[32]{0:T(128)S(1)}, s32[32]{0:T(128)}, u32[]{:S(2)}) copy-start(s32[32]{0:T(128)} %piece_slot.1) | copy-start | bytes 388

commit v3 on v2

--- a/solution.py
+++ b/solution.py
@@ -292,16 +292,20 @@
         if d == 0:
             return
         summed[d - 1] = mine[d] + from_sibling[d]
-        out = remote(
-            summed.at[d - 1],
-            reduced.at[d - 1],
-            sum_send_sem.at[1, d],
-            reduce_sem.at[d - 1],
-            at(zs, t, c),
-        )
-        out.start()
-        sends.append(out)
-        return out
+        pair = []
+        for h in range(2):
+            part = pl.ds(h * (rows // 2), rows // 2)
+            out = remote(
+                summed.at[d - 1, part],
+                reduced.at[d - 1, part],
+                sum_send_sem.at[1 + h, d],
+                reduce_sem.at[h, d - 1],
+                at(zs, t, c),
+            )
+            out.start()
+            sends.append(out)
+            pair.append(out)
+        return pair
 
     outs = []
     held = multiply(0)
@@ -315,52 +319,53 @@
     held = multiply(chips - 1)
     outs.append(pass_on(chips - 1, held))
 
-    total = mine[0] + from_sibling[0]
-    for d in range(1, chips):
-        outs[d - 1].wait_recv()
-        total = total + reduced[d - 1]
-    block = pl.ds(pl.multiple_of(z * rows, rows), rows)
-    fresh[c, block] = total.astype(jnp.bfloat16)
-    for d in range(1, chips):
-        copy = remote(
-            fresh.at[c, block],
-            fresh.at[c, block],
-            fresh_send_sem.at[0, d],
-            fresh_sem.at[z],
-            at(lax.rem(z + d, chips), t, c),
-        )
-        copy.start()
-        sends.append(copy)
-    for d in range(chips):
-        zs = lax.rem(z + chips - d, chips)
-        arrived = pl.ds(pl.multiple_of(zs * rows, rows), rows)
-        if d > 0:
+    size = rows // 2
+
+    def part_of(zs, h):
+        return pl.ds(pl.multiple_of(zs * rows + h * size, size), size)
+
+    for h in range(2):
+        part = slice(h * size, (h + 1) * size)
+        total = mine[0, part] + from_sibling[0, part]
+        for d in range(1, chips):
+            outs[d - 1][h].wait_recv()
+            total = total + reduced[d - 1, part]
+        fresh[c, part_of(z, h)] = total.astype(jnp.bfloat16)
+        block = fresh.at[c, part_of(z, h)]
+        for d in range(1, chips):
+            copy = remote(
+                block,
+                block,
+                fresh_send_sem.at[0, h, d],
+                fresh_sem.at[h, z],
+                at(lax.rem(z + d, chips), t, c),
+            )
+            copy.start()
+            sends.append(copy)
+    for h in range(2):
+        for d in range(chips):
+            zs = lax.rem(z + chips - d, chips)
+            block = fresh.at[c, part_of(zs, h)]
+            copy = remote(
+                block,
+                block,
+                fresh_send_sem.at[1, h, d],
+                fresh_sibling_sem.at[h, zs],
+                at(z, t, other),
+            )
+            if d > 0:
+                remote(
+                    block, block, send_sem.at[0], fresh_sem.at[h, zs], at(z, t, other)
+                ).wait_recv()
+            copy.start()
+            sends.append(copy)
+    for h in range(2):
+        for d in range(chips):
+            zs = lax.rem(z + chips - d, chips)
+            block = fresh.at[other, part_of(zs, h)]
             remote(
-                fresh.at[c, arrived],
-                fresh.at[c, arrived],
-                send_sem.at[0],
-                fresh_sem.at[zs],
-                at(z, t, other),
+                block, block, send_sem.at[0], fresh_sibling_sem.at[h, zs], at(z, t, other)
             ).wait_recv()
-        copy = remote(
-            fresh.at[c, arrived],
-            fresh.at[c, arrived],
-            fresh_send_sem.at[1, d],
-            fresh_sibling_sem.at[zs],
-            at(z, t, other),
-        )
-        copy.start()
-        sends.append(copy)
-    for d in range(chips):
-        zs = lax.rem(z + chips - d, chips)
-        arrived = pl.ds(pl.multiple_of(zs * rows, rows), rows)
-        remote(
-            fresh.at[other, arrived],
-            fresh.at[other, arrived],
-            send_sem.at[0],
-            fresh_sibling_sem.at[zs],
-            at(z, t, other),
-        ).wait_recv()
     for copy in sends:
         copy.wait_send()
 
@@ -392,14 +397,14 @@
             dma,
             dma((2 * chips - 1,)),
             dma((chips - 1, 2, planes - 1)),
-            dma((2, chips)),
-            dma((2, chips)),
+            dma((3, chips)),
+            dma((2, 2, chips)),
             dma((shards,)),
             dma((shards, planes)),
             dma((chips,)),
-            dma((chips - 1,)),
-            dma((chips,)),
-            dma((chips,)),
+            dma((2, chips - 1)),
+            dma((2, chips)),
+            dma((2, chips)),
         ],
         compiler_params=pltpu.CompilerParams(
             collective_id=0, has_side_effects=True, vmem_limit_bytes=40 * 2**20

time: 75.4 us -> 75.3 us (level); the launches traced: 75.2 us -> 73.9 us
  Pallas kernels: 72.6 us -> 71.2 us
    pallas_call x1, Pallas kernels: 57.2 us -> 56 us  [project(): pl.pallas_call(functools.partial(project_kernel, chips, planes), out_shap...]
where the time goes in v3:
time: 75.3 us; the launch traced here: 73.9 us
  Pallas kernels  71.2 us (95%)
  local copies, waits for them, and re-layouts  1.91 us (3%)
    pallas_call x1, Pallas kernels, project(): pl.pallas_call(functools.partial(project_kernel, chips, planes), out_shap...  56 us
    pallas_call x1, Pallas kernels, attend(): pl.pallas_call(functools.partial(attend_kernel, piece, shards), out_shape...  15.3 us
    unnamed x13, local copies, waits for them, and re-layouts  1.91 us

profile of v3, /device:TPU:9, one launch (start us, length us, event | category | flops | bytes accessed | tf_op | source)
XLA Modules:
  0.0 73.9 jit_solution(1666721879701439016)
XLA Ops:
  0.6 0.0 copy-start
  0.6 1.6 %copy.9 = bf16[128,8,2,256]{3,1,2,0:T(8,128)(2,1)S(1)} copy(bf16[128,8,2,256]{3,2,1,0:T(2,128)(2,1)} %bitcast.5) | data formatting | bytes 2097152
  2.2 0.3 copy-done
  2.5 0.0 copy-start.1
  2.5 0.0 copy-start.2
  2.5 0.0 copy-start.3
  2.5 0.0 copy-start.4
  2.5 0.0 copy-start.5
  2.6 56.0 %project.1.fresh = bf16[2,1024,256]{2,1,0:T(8,128)(2,1)S(1)} custom-call(bf16[4,32,8192]{2,1,0:T(8,128)(2,1)S(1)} %bitcast.4, bf16[1024,512]{1,0:T(8,128)(2,1)S(1)} %bitcast.3), custom_call_target="tpu_custom_call" | custom-call | tf_op jit(solution)/shard_map/project/pallas_call | solution.py:382
  58.6 0.0 copy-done.1
  58.6 0.0 copy-done.2
  58.6 0.0 copy-done.3
  58.6 0.0 copy-done.4
  58.6 0.0 copy-done.5
  58.6 15.3 %attend.1 = (bf16[256,2,256]{2,1,0:T(2,128)(2,1)}, bf16[256,2048]{1,0:T(8,128)(2,1)}) custom-call(s32[64]{0:T(128)S(1)} %copy-done.3, s32[32]{0:T(128)S(1)} %copy-done.4, s32[32]{0:T(128)S(1)} %copy-done.5, bf16[2,1024,256]{2,1,0:T(8,128)(2,1)S(1)} %project.1.fresh, bf16[256,2048]{1,0:T(8,128)(2,1)S(1)} %copy-done.1, bf16[256,2,256]{2,1,0:T(2,128)(2,1)S(1)} %copy-done.2), custom_call_target="tpu_custom_call" | custom-call | tf_op jit(solution)/shard_map/attend/pallas_call | solution.py:606
Async XLA Ops:
  0.6 1.9 %copy-start = (bf16[128,8192]{1,0:T(8,128)(2,1)S(1)}, bf16[128,8192]{1,0:T(8,128)(2,1)}, u32[]{:S(2)}) copy-start(bf16[128,8192]{1,0:T(8,128)(2,1)} %param.7) | copy-start | bytes 6291460
  2.5 56.0 %copy-start.1 = (bf16[256,2048]{1,0:T(8,128)(2,1)S(1)}, bf16[256,2048]{1,0:T(8,128)(2,1)}, u32[]{:S(2)}) copy-start(bf16[256,2048]{1,0:T(8,128)(2,1)} %queries.1) | copy-start | bytes 3145732
  2.5 56.0 %copy-start.2 = (bf16[256,2,256]{2,1,0:T(2,128)(2,1)S(1)}, bf16[256,2,256]{2,1,0:T(2,128)(2,1)}, u32[]{:S(2)}) copy-start(bf16[256,2,256]{2,1,0:T(2,128)(2,1)} %decode.1) | copy-start | bytes 786436
  2.5 56.0 %copy-start.3 = (s32[64]{0:T(128)S(1)}, s32[64]{0:T(128)}, u32[]{:S(2)}) copy-start(s32[64]{0:T(128)} %lengths.1) | copy-start | bytes 772
  2.5 56.0 %copy-start.4 = (s32[32]{0:T(128)S(1)}, s32[32]{0:T(128)}, u32[]{:S(2)}) copy-start(s32[32]{0:T(128)} %piece_owner.1) | copy-start | bytes 388
  2.5 56.1 %copy-start.5 = (s32[32]{0:T(128)S(1)}, s32[32]{0:T(128)}, u32[]{:S(2)}) copy-start(s32[32]{0:T(128)} %piece_slot.1) | copy-start | bytes 388
